TPU v7x, 128 devices: a whole 4x4x4 slice. The times are simulated.
128 devices in a mesh: energy: 4 (over x_lo, core), row: 8 (over x_hi, y), col: 4 (over z).
Axes of the slice: x: 4 (x_hi: 2, x_lo: 2; x = x_hi * 2 + x_lo), y: 4, z: 4, core: 2. Of those that a mesh axis runs over, the one named last changes fastest.
Arguments:
- green: bfloat16 [4, 2, 8192, 2048], P('energy', None, 'row', 'col'), may hold values from -0.890625 to 0.890625
- broadening: bfloat16 [4, 2, 2048, 2048], P('energy', None, None, 'col'), may hold values from -34 to 34, as said below
- quad_weight: float32 [4], P('energy'), may hold values from 0.25 to 1
- pair_cols: int32 [2048], P('row'), may hold values from 0 to 127, as said below
Outputs:
- density: float32 [8, 256, 64, 128], P('row', ('energy', 'col'))
Inputs may be any that keep to these rules, and one draw needn't show every extreme that they name: broadening[e] is exactly Hermitian (real part symmetric, imaginary part antisymmetric). `pair_cols`: pattern block q lies in slab s = q // 256, and its block column lies in slabs s - 1, s or s + 1 (block columns of slab t are t * 16 to (t + 1) * 16 - 1).
All inputs are finite; a program needn't handle non-finite values.
Results may differ from a plain program's by a relative error of at most 0.0018.
Values may be sent and summed in bfloat16 or wider, within the bound.
A program may use at most 128 MiB of HBM per device.

v0:
```python
import jax
import jax.numpy as jnp
from jax import lax
from jax.sharding import PartitionSpec as P


def with_halo(shard, sides, width):
    for axis, dim in sides:
        devices, length = (lax.axis_size(axis), shard.shape[dim])
        up = [(i, (i + 1) % devices) for i in range(devices - 1)]
        down = [(j, i) for i, j in up]
        last = lax.slice_in_dim(shard, length - width, length, axis=dim)
        first = lax.slice_in_dim(shard, 0, width, axis=dim)
        before = lax.ppermute(last, axis, up)
        after = lax.ppermute(first, axis, down)
        shard = jnp.concatenate([before, shard, after], axis=dim)
    return shard


def body(green, broadening, quad_weight, pair_cols):
    en_local = green.shape[0]
    rows = green.shape[2]
    cols_local = green.shape[3]
    block = 64
    blk_local = rows // block
    per_row = pair_cols.shape[0] // blk_local
    piece = lax.all_gather(green, "col", axis=3, tiled=True)
    gam_re = broadening[:, 0]
    gam_im = broadening[:, 1]
    part_re = jnp.einsum(
        "erk,ekc->erc", piece[:, 0], gam_re, preferred_element_type=jnp.float32
    ) - jnp.einsum("erk,ekc->erc", piece[:, 1], gam_im, preferred_element_type=jnp.float32)
    part_im = jnp.einsum(
        "erk,ekc->erc", piece[:, 0], gam_im, preferred_element_type=jnp.float32
    ) + jnp.einsum("erk,ekc->erc", piece[:, 1], gam_re, preferred_element_type=jnp.float32)
    spectral = jnp.stack([part_re, part_im], axis=1).astype(jnp.bfloat16)
    widened = with_halo(green, (("row", 2),), rows)
    near_blocks = widened.reshape(en_local, 2, 3 * blk_local, block, cols_local)
    spec_blocks = spectral.reshape(en_local, 2, blk_local, block, cols_local)
    first_block = (lax.axis_index("row") - 1) * blk_local
    local_cols = pair_cols.reshape(blk_local, per_row) - first_block

    def one_row(index):
        wanted = local_cols[index]
        taken = jnp.take(near_blocks, wanted, axis=2)
        left = lax.dynamic_index_in_dim(spec_blocks, index, 2, keepdims=False)
        real_part = jnp.einsum(
            "eam,ekcm->ekac", left[:, 0], taken[:, 0], preferred_element_type=jnp.float32
        ) + jnp.einsum(
            "eam,ekcm->ekac", left[:, 1], taken[:, 1], preferred_element_type=jnp.float32
        )
        imag_part = jnp.einsum(
            "eam,ekcm->ekac", left[:, 1], taken[:, 0], preferred_element_type=jnp.float32
        ) - jnp.einsum(
            "eam,ekcm->ekac", left[:, 0], taken[:, 1], preferred_element_type=jnp.float32
        )
        joined = jnp.concatenate([real_part, imag_part], axis=-1)
        return jnp.sum(quad_weight[:, None, None, None] * joined, axis=0)

    partial_blocks = lax.map(one_row, jnp.arange(blk_local, dtype=jnp.int32))
    partial_blocks = partial_blocks.reshape(blk_local * per_row, block, 2 * block)
    reduced = lax.psum_scatter(partial_blocks, ("energy", "col"), scatter_dimension=0, tiled=True)
    return reduced[None]


def solution(mesh):
    placed = (
        P("energy", None, "row", "col"),
        P("energy", None, None, "col"),
        P("energy"),
        P("row"),
    )
    return jax.shard_map(
        body,
        mesh=mesh,
        in_specs=placed,
        out_specs=P("row", ("energy", "col"), None, None),
        check_vma=False,
    )
```

profile of v0, /device:TPU:96, one launch (start us, length us, event | category | flops | bytes accessed | tf_op | source)
XLA Modules:
  0.0 397.5 jit_solution(7730755887078647196)
XLA Ops:
  8.1 4.8 %collective-permute-start = (bf16[1,2,1024,512]{3,2,1,0:T(8,128)(2,1)S(1)}, bf16[1,2,1024,512]{3,2,1,0:T(8,128)(2,1)}, u32[]{:S(2)}, u32[]{:S(2)}) collective-permute-start(bf16[1,2,1024,512]{3,2,1,0:T(8,128)(2,1)S(1)} %copy-done), channel_id=1, source_target_pairs={{0,4},{4,8},{8,12},{12,16},{16,20},{20,24},{24,28},{1,5},{5,9},{9,... | collective-permute-start | bytes 6291464 | tf_op jit(solution)/shard_map/ppermute | solution.py:14
  14.4 42.1 %collective-permute-done = bf16[1,2,1024,512]{3,2,1,0:T(8,128)(2,1)} collective-permute-done((bf16[1,2,1024,512]{3,2,1,0:T(8,128)(2,1)S(1)}, bf16[1,2,1024,512]{3,2,1,0:T(8,128)(2,1)}, u32[]{:S(2)}, u32[]{:S(2)}) %collective-permute-start) | collective-permute-done | bytes 2097184 | tf_op jit(solution)/shard_map/ppermute | solution.py:14
  56.5 5.6 %collective-permute-done.1 = bf16[1,2,1024,512]{3,2,1,0:T(8,128)(2,1)} collective-permute-done((bf16[1,2,1024,512]{3,2,1,0:T(8,128)(2,1)S(1)}, bf16[1,2,1024,512]{3,2,1,0:T(8,128)(2,1)}, u32[]{:S(2)}, u32[]{:S(2)}) %collective-permute-start.1) | collective-permute-done | bytes 2097184 | tf_op jit(solution)/shard_map/ppermute | solution.py:15
  62.0 5.4 %pad_maximum_fusion = bf16[1,2,3072,512]{3,2,1,0:T(8,128)(2,1)} fusion(bf16[1,2,1024,512]{3,2,1,0:T(8,128)(2,1)} %collective-permute-done.1, bf16[1,2,1024,512]{3,2,1,0:T(8,128)(2,1)S(1)} %copy-done, bf16[1,2,1024,512]{3,2,1,0:T(8,128)(2,1)} %collective-permute-done), kind=kLoop, calls=%fused_computation.21 | loop fusion | flops 18874368 | bytes 12582912 | tf_op jit(solution)/shard_map/concatenate | solution.py:16
  67.4 24.6 %all-gather.2.cloned.1.call-done = bf16[1,2,1024,2048]{3,2,1,0:T(8,128)(2,1)} async-done(((bf16[1,2,1024,512]{3,2,1,0:T(8,128)(2,1)}), bf16[1,2,1024,2048]{3,2,1,0:T(8,128)(2,1)}) %all-gather.2.cloned.1.call-update) | async-done | bytes 8388624 | tf_op jit(solution)/shard_map/all_gather | solution.py:27
  92.0 5.3 %fusion.7 = f32[1024,512]{1,0:T(8,128)S(1)} fusion(bf16[1,2,1024,2048]{3,2,1,0:T(8,128)(2,1)} %all-gather.2.cloned.1.call-done, bf16[1,2,2048,512]{3,2,1,0:T(8,128)(2,1)} %param.7), kind=kOutput, calls=%fused_computation.25 | convolution fusion | flops 2147483648 | bytes 8388608 | tf_op jit(solution)/shard_map/erk,ekc->erc/dot_general | solution.py:30
  98.5 2.3 fusion.6
  100.8 2.3 subtract_convert_fusion
  103.1 2.3 add_convert_fusion
  107.0 184.9 %while.10 = (s32[]{:T(128)}, f32[16,16,64,128]{3,2,1,0:T(8,128)}, f32[1]{0:T(128)}, s32[16]{0:T(128)S(1)}, s32[16,16]{1,0:T(8,128)S(1)}, /*index=5*/bf16[1,2,48,...) while((s32[]{:T(128)}, f32[16,16,64,128]{3,2,1,0:T(8,128)}, ...), condition=%wide.region_1.2_spmd, body=%wide.region_0.1_spmd.sunk | while | flops 269878400 | bytes 16258559 | solution.py:60
  109.7 3.5 gather_fusion
  116.9 1.7 fusion.33
  121.3 3.5 gather_fusion
  128.4 1.7 fusion.33
  132.9 3.5 gather_fusion
  144.4 3.5 gather_fusion
  155.9 3.5 gather_fusion
  163.1 1.7 fusion.33
  167.5 3.5 gather_fusion
  179.1 3.5 gather_fusion
  190.6 3.5 gather_fusion
  202.1 3.5 gather_fusion
  213.7 3.5 gather_fusion
  220.9 1.7 fusion.33
  225.3 3.5 gather_fusion
  236.8 3.5 gather_fusion
  248.4 3.5 gather_fusion
  259.9 3.5 gather_fusion
  271.5 3.5 gather_fusion
  278.7 1.7 fusion.33
  283.0 3.5 gather_fusion
  291.9 98.7 %reduce-scatter.2.cloned.1.call-done = f32[16,64,128]{2,1,0:T(8,128)} async-done(((f32[256,64,128]{2,1,0:T(8,128)}), f32[16,64,128]{2,1,0:T(8,128)}) %reduce-scatter.2.cloned.1.call-update) | async-done | bytes 524304 | tf_op jit(solution)/shard_map/reduce_scatter | solution.py:62
  (189 shorter events, 93.6 us)
Async XLA Ops:
  6.5 1.6 copy-start
  6.5 7.7 %copy-start.1 = (s32[256]{0:T(256)S(1)}, s32[256]{0:T(256)}, u32[]{:S(2)}) copy-start(s32[256]{0:T(256)} %param.9) | copy-start | bytes 3076
  6.5 85.5 %all-gather.2.cloned.1.call-start = ((), (), s32[]{:S(2)}) async-start(), calls=%async_computation.1 | async-start | bytes 10485760 | tf_op jit(solution)/shard_map/all_gather | solution.py:27
  7.3 383.4 %reduce-scatter.2.cloned.1.call-start = ((), (), s32[]{:S(2)}) async-start(), calls=%async_computation.2 | async-start | bytes 8912896 | tf_op jit(solution)/shard_map/reduce_scatter | solution.py:62
  8.1 48.3 %collective-permute-start = (bf16[1,2,1024,512]{3,2,1,0:T(8,128)(2,1)S(1)}, bf16[1,2,1024,512]{3,2,1,0:T(8,128)(2,1)}, u32[]{:S(2)}, u32[]{:S(2)}) collective-permute-start(bf16[1,2,1024,512]{3,2,1,0:T(8,128)(2,1)S(1)} %copy-done), channel_id=1, source_target_pairs={{0,4},{4,8},{8,12},{12,16},{16,20},{20,24},{24,28},{1,5},{5,9},{9,... | collective-permute-start | bytes 6291464 | tf_op jit(solution)/shard_map/ppermute | solution.py:14
  13.0 49.1 %collective-permute-start.1 = (bf16[1,2,1024,512]{3,2,1,0:T(8,128)(2,1)S(1)}, bf16[1,2,1024,512]{3,2,1,0:T(8,128)(2,1)}, u32[]{:S(2)}, u32[]{:S(2)}) collective-permute-start(bf16[1,2,1024,512]{3,2,1,0:T(8,128)(2,1)S(1)} %copy-done), channel_id=1, source_target_pairs={{4,0},{8,4},{12,8},{16,12},{20,16},{24,20},{28,24},{5,1},{9,5},{13... | collective-permute-start | bytes 6291464 | tf_op jit(solution)/shard_map/ppermute | solution.py:15
  92.0 5.3 %copy-start.2 = (bf16[1,2,1024,2048]{3,2,1,0:T(8,128)(2,1)S(1)}, bf16[1,2,1024,2048]{3,2,1,0:T(8,128)(2,1)}, u32[]{:S(2)}) copy-start(bf16[1,2,1024,2048]{3,2,1,0:T(8,128)(2,1)} %all-gather.2.cloned.1.call-done) | copy-start | bytes 25165828
  92.0 6.4 %copy-start.3 = (bf16[1,2,2048,512]{3,2,1,0:T(8,128)(2,1)S(1)}, bf16[1,2,2048,512]{3,2,1,0:T(8,128)(2,1)}, u32[]{:S(2)}) copy-start(bf16[1,2,2048,512]{3,2,1,0:T(8,128)(2,1)} %param.7) | copy-start | bytes 12582916
Sparse Core Ops, SparseCore 0:
  9.0 82.9 all-gather.1
  292.0 98.5 reduce-scatter.1
where the time goes:
time: 403 us; the launch traced here: 398 us
  waiting for transfers between devices  172 us (43%)
  local copies, waits for them, and re-layouts  82.5 us (20%)
  matrix products  52.1 us (13%)
  other arithmetic  38.4 us (10%)
  loops' own time  33 us (8%)
  between operations  13.5 us (3%)
  starting transfers between devices  6.16 us (2%)
    reduce_scatter x1, waiting for transfers between devices, body(): lax.psum_scatter(partial_blocks, ('energy', 'col'), scatter_dimension=0,...  98.7 us
    gather x16, local copies, waits for them, and re-layouts, one_row(): taken = jnp.take(near_blocks, wanted, axis=2)  55.5 us
    ppermute x1, waiting for transfers between devices, with_halo(): before = lax.ppermute(last, axis, up)  42.1 us
    another operation x1, loops' own time, body(): partial_blocks = lax.map(one_row, jnp.arange(blk_local, dtype=jnp.int32))  33 us
    dynamic_update_slice x16, other arithmetic, body(): partial_blocks = lax.map(one_row, jnp.arange(blk_local, dtype=jnp.int32))  26.7 us
    all_gather x1, waiting for transfers between devices, body(): piece = lax.all_gather(green, 'col', axis=3, tiled=True)  24.6 us
    squeeze x16, local copies, waits for them, and re-layouts, one_row(): left = lax.dynamic_index_in_dim(spec_blocks, index, 2, keepdims=False)  14.7 us
    dynamic_slice x16, local copies, waits for them, and re-layouts, body(): partial_blocks = lax.map(one_row, jnp.arange(blk_local, dtype=jnp.int32))  10.3 us
  transfers between devices with their start and end apart: 4, of which 4 were waited for; matrix products, arithmetic and copies ran while one was open for 1% of the time, Pallas kernels for 0%

commit v1 on v0

v1 whole, which is shorter than its diff:
```python
import functools

import jax
import jax.numpy as jnp
from jax import lax
from jax.experimental import pallas as pl
from jax.experimental.pallas import tpu as pltpu
from jax.sharding import PartitionSpec as P

MESH = pl.DeviceIdType.MESH
NT = (((1,), (1,)), ((), ()))
BLOCK = 64
PB = 16
TOP = 32766.0
CHUNKS = 8
LEAD = 2


def encode(total, codes, scale):
    peak = jnp.maximum(jnp.max(jnp.abs(total), axis=0, keepdims=True), 1e-30)
    codes[...] = jnp.round(total * (TOP / peak)).astype(jnp.int32).astype(jnp.int16)
    scale[...] = jnp.broadcast_to(peak * (1.0 / TOP), scale.shape)


def decode(codes, scale):
    return codes[...].astype(jnp.int32).astype(jnp.float32) * scale[0:1, :]


def kernel(
    green, gamma, weight, pairs, out,
    gall, near, gam, spec, csend, crecv, xsend, xrecv, xsscale, xrscale, zsend, zrecv, zsscale, zrscale, own,
    loc, gs, gr, rs, rr, ys, yr, cs, cr, xs, xr, xss, xrs, zs, zr, zss, zrs,
):
    e, r, c = lax.axis_index("energy"), lax.axis_index("row"), lax.axis_index("col")
    xbit, core = e // 2, e % 2
    up, down, over = (c + 1) % 4, (c + 3) % 4, (c + 2) % 4
    above, below = (r + 1) % 8, (r + 7) % 8
    core_peer, x_peer = (e + 1 - 2 * core, r, c), (e + 2 - 4 * xbit, r, c)
    z_up, z_down = (e, r, up), (e, r, down)

    def cols(owner):
        return pl.ds(pl.multiple_of(owner * 512, 512), 512)

    def block_of(u, half):
        dx, kp, dk = 1 - u // 4, (u // 2) % 2, 1 - u % 2
        return ((xbit + dx) % 2) * 8 + ((core + dk) % 2) * 4 + kp * 2 + half

    def rows_of(u, half=0, count=2):
        return pl.ds(block_of(u, half), count)

    def remote(src, dst, send, recv, peer):
        return pltpu.make_async_remote_copy(
            src_ref=src, dst_ref=dst, send_sem=send, recv_sem=recv, device_id=peer, device_id_type=MESH
        )

    def hand(u, way):
        return remote(
            green.at[0, :, rows_of(u)], gall.at[:, rows_of(u), :, cols(c)],
            gs.at[way, u], gr.at[way, u], (z_up, z_down)[way],
        )

    def handed(u, way):
        origin = (down, up)[way]
        return remote(
            green.at[0, :, rows_of(u)], gall.at[:, rows_of(u), :, cols(origin)],
            gs.at[way, u], gr.at[way, u], (z_up, z_down)[way],
        )

    def relay(u, way):
        piece = gall.at[:, rows_of(u, way, 1), :, cols((down, up)[way])]
        return remote(piece, piece, rs.at[way, u], rr.at[way, u], (z_up, z_down)[way])

    def relayed(u, way):
        piece = gall.at[:, rows_of(u, way, 1), :, cols(over)]
        return remote(piece, piece, rs.at[way, u], rr.at[way, u], (z_up, z_down)[way])

    def halo(way):
        return remote(
            green.at[0], near.at[:, pl.ds(32 * way, 16)], ys.at[way], yr.at[way],
            (e, (above, below)[way], c),
        )

    def core_copy(n):
        return remote(csend.at[n], crecv.at[n], cs.at[n], cr.at[n], core_peer)

    def x_copies(n):
        return (
            remote(xsend.at[n], xrecv.at[n], xs.at[n], xr.at[n], x_peer),
            remote(xsscale.at[n], xrscale.at[n], xss.at[n], xrs.at[n], x_peer),
        )

    def z_copies(k, slot):
        return (
            remote(zsend.at[k], zrecv.at[slot], zs.at[k], zr.at[slot], (e, r, k)),
            remote(zsscale.at[k], zrscale.at[slot], zss.at[k], zrs.at[slot], (e, r, k)),
        )

    locals_ = [
        pltpu.make_async_copy(green.at[0], gall.at[:, :, :, cols(c)], loc.at[0]),
        pltpu.make_async_copy(gamma.at[0], gam, loc.at[1]),
        pltpu.make_async_copy(green.at[0], near.at[:, pl.ds(16, 16)], loc.at[2]),
    ]
    for copy in locals_:
        copy.start()

    barrier = pltpu.get_barrier_semaphore()
    peers = (core_peer, x_peer, z_up, z_down, (e, r, over), (e, above, c), (e, below, c))
    for peer in peers:
        pl.semaphore_signal(barrier, inc=1, device_id=peer, device_id_type=MESH)
    pl.semaphore_wait(barrier, len(peers))

    for u in range(LEAD):
        for way in range(2):
            hand(u, way).start()
    for way in range(2):
        halo(way).start()
    for copy in locals_:
        copy.wait()

    def feed(t):
        @pl.when(t < CHUNKS - LEAD)
        def _():
            for way in range(2):
                hand(t + LEAD, way).start()

        @pl.when(t < CHUNKS)
        def _():
            for way in range(2):
                handed(t, way).wait_recv()
                relay(t, way).start()

    def spectral(u):
        for way in range(2):
            relayed(u, way).wait_recv()
        first = block_of(u, 0)
        left = gall[:, rows_of(u)].reshape(256, 2048)
        with_re = jnp.dot(left, gam[0], preferred_element_type=jnp.float32)
        with_im = jnp.dot(left, gam[1], preferred_element_type=jnp.float32)
        re = (with_re[:128] - with_im[128:]).astype(jnp.bfloat16)
        im = (with_im[:128] + with_re[128:]).astype(jnp.bfloat16)
        for half in range(2):
            a, b = re[half * BLOCK : (half + 1) * BLOCK], im[half * BLOCK : (half + 1) * BLOCK]
            spec[first + half, 0:BLOCK, 0:512] = a
            spec[first + half, 0:BLOCK, 512:1024] = b
            spec[first + half, BLOCK:128, 0:512] = b
            spec[first + half, BLOCK:128, 512:1024] = -a

    def terms(u, half):
        block = block_of(u, half)
        at = [jnp.clip(pairs[block * PB + p] - (r - 1) * PB, 0, 47) for p in range(PB)]
        right_re = jnp.concatenate([near[0, o] for o in at], axis=0)
        right_im = jnp.concatenate([near[1, o] for o in at], axis=0)
        left = spec[block]
        found = lax.dot_general(right_re, left[:, :512], NT, preferred_element_type=jnp.float32)
        found += lax.dot_general(right_im, left[:, 512:], NT, preferred_element_type=jnp.float32)
        return found * weight[0]

    def step(t, carry):
        feed(t)

        @pl.when(t > 0)
        def _():
            spectral(t - 1)

        return carry

    lax.fori_loop(0, 5, step, 0)
    for way in range(2):
        halo(way).wait_recv()

    def late_step(g, carry):
        feed(g + 5)
        spectral(g + 4)

        def give(half, inner):
            n = g * 2 + half
            csend[n] = terms(2 * g, half)
            core_copy(n).start()
            return inner

        lax.fori_loop(0, 2, give, 0)

        def keep(half, inner):
            n = g * 2 + half
            mine = terms(2 * g + 1, half)
            core_copy(n).wait_recv()
            total = mine + crecv[n]

            @pl.when(g < 2)
            def _():
                encode(total, xsend.at[n], xsscale.at[n])
                for copy in x_copies(n):
                    copy.start()

            @pl.when(g >= 2)
            def _():
                k = n - 4
                for copy in x_copies(k):
                    copy.wait_recv()
                both = total + decode(xrecv[k], xrscale[k])

                @pl.when(k == c)
                def _():
                    own[...] = both

                @pl.when(k != c)
                def _():
                    encode(both, zsend.at[k], zsscale.at[k])
                    for copy in z_copies(k, (c - k + 3) % 4):
                        copy.start()

            return inner

        lax.fori_loop(0, 2, keep, 0)
        return carry

    lax.fori_loop(0, 4, late_step, 0)

    total = own[...]
    for slot in range(3):
        for copy in z_copies((c + 1) % 4, slot):
            copy.wait_recv()
        total = total + decode(zrecv[slot], zrscale[slot])
    own[...] = total
    for p in range(PB):
        turned = own[p * BLOCK : (p + 1) * BLOCK, :].T
        out[0, p, :, 0:BLOCK] = turned[0:BLOCK]
        out[0, p, :, BLOCK:128] = turned[BLOCK:128]

    def sent(u, carry):
        for way in range(2):
            hand(u, way).wait_send()
            relay(u, way).wait_send()
        core_copy(u).wait_send()
        return carry

    lax.fori_loop(0, CHUNKS, sent, 0)
    for way in range(2):
        halo(way).wait_send()
    for n in range(4):
        for copy in x_copies(n):
            copy.wait_send()
    for step_ in range(1, 4):
        for copy in z_copies((c + step_) % 4, 0):
            copy.wait_send()


def body(green, broadening, quad_weight, pair_cols):
    vmem, smem = pl.BlockSpec(memory_space=pltpu.VMEM), pl.BlockSpec(memory_space=pltpu.SMEM)
    hbm = pl.BlockSpec(memory_space=pl.ANY)
    dma = pltpu.SemaphoreType.DMA
    return pl.pallas_call(
        kernel,
        out_shape=jax.ShapeDtypeStruct((1, PB, BLOCK, 2 * BLOCK), jnp.float32),
        in_specs=[hbm, hbm, smem, smem],
        out_specs=vmem,
        scratch_shapes=[
            pltpu.VMEM((2, 16, BLOCK, 2048), jnp.bfloat16),
            pltpu.VMEM((2, 48, BLOCK, 512), jnp.bfloat16),
            pltpu.VMEM((2, 2048, 512), jnp.bfloat16),
            pltpu.VMEM((16, 128, 1024), jnp.bfloat16),
            pltpu.VMEM((8, 1024, 128), jnp.float32),
            pltpu.VMEM((8, 1024, 128), jnp.float32),
            pltpu.VMEM((4, 1024, 128), jnp.int16),
            pltpu.VMEM((4, 1024, 128), jnp.int16),
            pltpu.VMEM((4, 8, 128), jnp.float32),
            pltpu.VMEM((4, 8, 128), jnp.float32),
            pltpu.VMEM((4, 1024, 128), jnp.int16),
            pltpu.VMEM((3, 1024, 128), jnp.int16),
            pltpu.VMEM((4, 8, 128), jnp.float32),
            pltpu.VMEM((3, 8, 128), jnp.float32),
            pltpu.VMEM((1024, 128), jnp.float32),
            dma((3,)),
            dma((2, CHUNKS)), dma((2, CHUNKS)), dma((2, CHUNKS)), dma((2, CHUNKS)),
            dma((2,)), dma((2,)),
            dma((8,)), dma((8,)),
            dma((4,)), dma((4,)), dma((4,)), dma((4,)),
            dma((4,)), dma((3,)), dma((4,)), dma((3,)),
        ],
        compiler_params=pltpu.CompilerParams(
            collective_id=0, has_side_effects=True, vmem_limit_bytes=56 * 1024 * 1024
        ),
        cost_estimate=pl.CostEstimate(flops=13 * 10**9, bytes_accessed=7 * 2**20, transcendentals=0),
        name="density",
    )(green.reshape(1, 2, 16, BLOCK, 512), broadening, quad_weight, pair_cols)


def solution(mesh):
    placed = (
        P("energy", None, "row", "col"),
        P("energy", None, None, "col"),
        P("energy"),
        P("row"),
    )
    return jax.shard_map(
        body,
        mesh=mesh,
        in_specs=placed,
        out_specs=P("row", ("energy", "col"), None, None),
        check_vma=False,
    )
```

time: 403 us -> 111 us (0.28); the launches traced: 398 us -> 110 us
  waiting for transfers between devices: 172 us -> 0 us
  Pallas kernels: 0 us -> 107 us
  local copies, waits for them, and re-layouts: 82.5 us -> 1.89 us
  matrix products: 52.1 us -> 0 us
  other arithmetic: 38.4 us -> 0 us
  loops' own time: 33 us -> 0 us
  between operations: 13.5 us -> 0.66 us
  starting transfers between devices: 6.16 us -> 0 us
    pallas_call x0 -> x1, Pallas kernels: none -> 107 us  [body(): pl.pallas_call(kernel, out_shape=jax.ShapeDtypeStruct((1, PB, BLOCK, 2 *...]
    reduce_scatter x1 -> x0, waiting for transfers between devices: 98.7 us -> none  [body(): lax.psum_scatter(partial_blocks, ('energy', 'col'), scatter_dimension=0,...]
    gather x16 -> x0, local copies, waits for them, and re-layouts: 55.5 us -> none  [one_row(): taken = jnp.take(near_blocks, wanted, axis=2)]
    dot_general x68 -> x0, matrix products: 52.1 us -> none  [the longest x16 9.99 us: one_row(): jnp.einsum('eam,ekcm->ekac', left[:, 1], taken[:, 1], preferred_element_t...]
    ppermute x2 -> x0, waiting for transfers between devices: 47.7 us -> none  [the longest x1 42.1 us: with_halo(): before = lax.ppermute(last, axis, up)]
    another operation x1 -> x0, loops' own time: 33 us -> none  [body(): partial_blocks = lax.map(one_row, jnp.arange(blk_local, dtype=jnp.int32))]
    dynamic_update_slice x16 -> x0, other arithmetic: 26.7 us -> none  [body(): partial_blocks = lax.map(one_row, jnp.arange(blk_local, dtype=jnp.int32))]
    all_gather x1 -> x0, waiting for transfers between devices: 24.6 us -> none  [body(): piece = lax.all_gather(green, 'col', axis=3, tiled=True)]
  transfers between devices with their start and end apart: 4 -> 0, of which waited for: 4 -> 0; matrix products, arithmetic and copies ran while one was open for 1% -> 0% of each run, Pallas kernels for 0% -> 0%
where the time goes in v1:
time: 111 us; the launch traced here: 110 us
  Pallas kernels  107 us (96%)
  local copies, waits for them, and re-layouts  1.89 us (2%)
    pallas_call x1, Pallas kernels, body(): pl.pallas_call(kernel, out_shape=jax.ShapeDtypeStruct((1, PB, BLOCK, 2 *...  107 us

profile of v1, /device:TPU:96, one launch (start us, length us, event | category | flops | bytes accessed | tf_op | source)
XLA Modules:
  0.0 109.9 jit_solution(17578625092974300911)
XLA Ops:
  0.7 107.3 %density.1 = f32[1,16,64,128]{3,2,1,0:T(8,128)} custom-call(bf16[1,2,16,64,512]{4,3,2,1,0:T(8,128)(2,1)} %bitcast.1, bf16[1,2,2048,512]{3,2,1,0:T(8,128)(2,1)} %gamma.1, f32[1]{0:T(128)S(6)} %copy.6.weight, s32[256]{0:T(256)} %pairs.1), custom_call_target="tpu_custom_call" | custom-call | flops 12999999488 | bytes 7340032 | tf_op jit(solution)/shard_map/density/pallas_call | solution.py:252
  108.0 1.9 %copy.7 = f32[1,16,64,128]{3,2,1,0:T(8,128)} copy(f32[1,16,64,128]{3,2,1,0:T(8,128)} %density.1) | data formatting | bytes 1048576

commit v2 on v1

v2 whole, which is shorter than its diff:
```python
import functools

import jax
import jax.numpy as jnp
from jax import lax
from jax.experimental import pallas as pl
from jax.experimental.pallas import tpu as pltpu
from jax.sharding import PartitionSpec as P

MESH = pl.DeviceIdType.MESH
NT = (((1,), (1,)), ((), ()))
BLOCK = 64
PB = 16
TOP = 32766.0
STEPS = 16
LEAD = 3
EARLY = 11


def scaled(total, peak):
    peak = jnp.maximum(peak, 1e-30)
    return total * (TOP / peak), peak * (1.0 / TOP)


def coded(values):
    return jnp.round(values).astype(jnp.int32).astype(jnp.int16)


def encode(total, codes, scale):
    values, unit = scaled(total, jnp.max(jnp.abs(total), axis=0, keepdims=True))
    codes[...] = coded(values)
    scale[...] = jnp.broadcast_to(unit, scale.shape)


def decode(codes, scale):
    return codes[...].astype(jnp.int32).astype(jnp.float32) * scale[0:1, :]


def kernel(
    green, gamma, weight, pairs, out,
    held, near_a, near_b, begun, mine, theirs, turn, given, spec, psend, precv, psscale, prscale,
    csend, crecv, xsend, xrecv, xsscale, xrscale, zsend, zrecv, zsscale, zrscale, own,
    loc, ws, wr, gs, gr, ps, pr, pss, prs, ys, yr, cs, cr, xs, xr, xss, xrs, zs, zr, zss, zrs,
):
    near = (near_a, near_b)
    e, r, c = lax.axis_index("energy"), lax.axis_index("row"), lax.axis_index("col")
    xbit, core = e // 2, e % 2
    pair, cross = c + 1 - 2 * (c % 2), 3 - c
    above, below = (r + 1) % 8, (r + 7) % 8
    core_peer, x_peer = (e + 1 - 2 * core, r, c), (e + 2 - 4 * xbit, r, c)
    pair_peer, cross_peer = (e, r, pair), (e, r, cross)

    def quarter(owner, count=512):
        return pl.ds(pl.multiple_of(owner * 512, 512), count)

    def block_of(u):
        dx, dk, k = 1 - u // 8, 1 - u % 2, (u % 8) // 2
        return ((xbit + dx) % 2) * 8 + ((core + dk) % 2) * 4 + k

    def remote(src, dst, send, recv, peer):
        return pltpu.make_async_remote_copy(
            src_ref=src, dst_ref=dst, send_sem=send, recv_sem=recv, device_id=peer, device_id_type=MESH
        )

    def hand(u):
        b = block_of(u)
        return remote(
            green.at[0, :, b], held.at[:, b, :, pl.ds(512, 512)], gs.at[u], gr.at[u], cross_peer
        )

    def weights():
        return (
            remote(gamma.at[0, :, quarter(3 - pair, 256), :], given, ws.at[0], wr.at[0], cross_peer),
            remote(
                gamma.at[0, :, quarter(3 - pair), pl.ds(256, 256)],
                theirs.at[:, pl.ds(512, 512), pl.ds(256, 256)], ws.at[1], wr.at[1], pair_peer,
            ),
        )

    def part_copies(u):
        return (
            remote(psend.at[u], precv.at[u], ps.at[u], pr.at[u], pair_peer),
            remote(psscale.at[u], prscale.at[u], pss.at[u], prs.at[u], pair_peer),
        )

    def halo(way, part):
        return remote(
            green.at[0, :, :, :, pl.ds(256 * part, 256)], near[part].at[:, pl.ds(32 * way, 16)],
            ys.at[way, part], yr.at[way, part], (e, (above, below)[way], c),
        )

    def core_copy(n):
        return remote(csend.at[n], crecv.at[n], cs.at[n], cr.at[n], core_peer)

    def x_copies(n):
        return (
            remote(xsend.at[n], xrecv.at[n], xs.at[n], xr.at[n], x_peer),
            remote(xsscale.at[n], xrscale.at[n], xss.at[n], xrs.at[n], x_peer),
        )

    def z_copies(k, slot):
        return (
            remote(zsend.at[k], zrecv.at[slot], zs.at[k], zr.at[slot], (e, r, k)),
            remote(zsscale.at[k], zrscale.at[slot], zss.at[k], zrs.at[slot], (e, r, k)),
        )

    locals_ = [
        pltpu.make_async_copy(gamma.at[0, :, quarter(pair), :], turn, loc.at[0]),
        pltpu.make_async_copy(gamma.at[0, :, quarter(c), :], mine.at[:, pl.ds(0, 512), :], loc.at[1]),
        pltpu.make_async_copy(gamma.at[0, :, quarter(cross), :], mine.at[:, pl.ds(512, 512), :], loc.at[2]),
        pltpu.make_async_copy(green.at[0], held.at[:, :, :, pl.ds(0, 512)], loc.at[3]),
        pltpu.make_async_copy(green.at[0, :, :, :, pl.ds(0, 256)], near_a.at[:, pl.ds(16, 16)], loc.at[4]),
        pltpu.make_async_copy(green.at[0, :, :, :, pl.ds(256, 256)], near_b.at[:, pl.ds(16, 16)], loc.at[5]),
    ]
    for copy in locals_:
        copy.start()

    barrier = pltpu.get_barrier_semaphore()
    peers = (core_peer, x_peer, pair_peer, cross_peer, (e, r, (c + 2) % 4), (e, above, c), (e, below, c))
    for peer in peers:
        pl.semaphore_signal(barrier, inc=1, device_id=peer, device_id_type=MESH)
    pl.semaphore_wait(barrier, len(peers))

    for copy in weights():
        copy.start()
    for u in range(LEAD):
        hand(u).start()
    for way in range(2):
        halo(way, 0).start()
    for copy in locals_:
        copy.wait()
    theirs[0, 0:512, :] = turn[0].T
    theirs[1, 0:512, :] = -(turn[1].T)
    for copy in weights():
        copy.wait_recv()
    theirs[0, 512:1024, 0:256] = given[0].T
    theirs[1, 512:1024, 0:256] = -(given[1].T)

    def product(b, right):
        left = held[:, b].reshape(2 * BLOCK, 1024)
        with_re = jnp.dot(left, right[0], preferred_element_type=jnp.float32)
        with_im = jnp.dot(left, right[1], preferred_element_type=jnp.float32)
        return jnp.concatenate(
            [with_re[:BLOCK] - with_im[BLOCK:], with_im[:BLOCK] + with_re[BLOCK:]], axis=1
        )

    def forward(u):
        @pl.when(u < STEPS - LEAD)
        def _():
            hand(u + LEAD).start()

        hand(u).wait_recv()
        part = product(block_of(u), theirs)
        peak = jnp.max(jnp.abs(part), axis=0, keepdims=True)
        peak = functools.reduce(jnp.maximum, [peak[:, 128 * i : 128 * (i + 1)] for i in range(8)])
        wide = jnp.concatenate([peak] * 8, axis=1)
        values, unit = scaled(part, wide)
        psend[u] = coded(values)
        psscale[u] = jnp.broadcast_to(unit[:, 0:128], (8, 128))
        for copy in part_copies(u):
            copy.start()

    def spectral(u):
        b = block_of(u)
        part = product(b, mine)
        for copy in part_copies(u):
            copy.wait_recv()
        unit = jnp.concatenate([prscale[u][0:1, :]] * 8, axis=1)
        whole = part + precv[u].astype(jnp.int32).astype(jnp.float32) * unit
        whole = whole.astype(jnp.bfloat16)
        spec[b, 0:BLOCK, :] = whole
        spec[b, BLOCK:128, 0:512] = whole[:, 512:]
        spec[b, BLOCK:128, 512:1024] = -whole[:, :512]

    def terms(dx, dk, k, part):
        block = ((xbit + dx) % 2) * 8 + ((core + dk) % 2) * 4 + k
        at = [jnp.clip(pairs[block * PB + p] - (r - 1) * PB, 0, 47) for p in range(PB)]
        right_re = jnp.concatenate([near[part][0, o] for o in at], axis=0)
        right_im = jnp.concatenate([near[part][1, o] for o in at], axis=0)
        left_re = spec[block, :, 256 * part : 256 * part + 256]
        left_im = spec[block, :, 512 + 256 * part : 768 + 256 * part]
        found = lax.dot_general(right_re, left_re, NT, preferred_element_type=jnp.float32)
        return found + lax.dot_general(right_im, left_im, NT, preferred_element_type=jnp.float32)

    def both(dx, dk, k):
        n = 2 * k + 1 - dk
        first = begun[n] if dx else terms(dx, dk, k, 0)
        return (first + terms(dx, dk, k, 1)) * weight[0]

    def give(dx, k):
        n = (1 - dx) * 4 + k
        csend[n] = both(dx, 1, k)
        core_copy(n).start()

    def kept(dx, k):
        n = (1 - dx) * 4 + k
        found = both(dx, 0, k)
        core_copy(n).wait_recv()
        return found + crecv[n]

    def class_of(s):
        return jnp.where(s == 3, c, jnp.where(s < c, s, s + 1))

    def step(u, carry):
        @pl.when(u < STEPS)
        def _():
            forward(u)

        @pl.when(u > 1)
        def _():
            spectral(u - 2)

        return carry

    def step_and_begin(u, carry):
        step(u, carry)
        n = u - 3
        begun[n] = terms(1, 1 - n % 2, n // 2, 0)
        return carry

    lax.fori_loop(0, 2, step, 0)
    for way in range(2):
        halo(way, 1).start()
    lax.fori_loop(2, 3, step, 0)
    for way in range(2):
        halo(way, 0).wait_recv()
    lax.fori_loop(3, EARLY, step_and_begin, 0)
    for way in range(2):
        halo(way, 1).wait_recv()
    give(1, class_of(0))

    def early(s, carry):
        k = class_of(s)

        @pl.when(s < 3)
        def _():
            give(1, class_of(s + 1))

        encode(kept(1, k), xsend.at[k], xsscale.at[k])
        for copy in x_copies(k):
            copy.start()
        return step(EARLY + s, carry)

    lax.fori_loop(0, 4, early, 0)

    def last(s):
        k = class_of(s)
        total = kept(0, k)
        for copy in x_copies(k):
            copy.wait_recv()
        return total + decode(xrecv[k], xrscale[k])

    def hand_in(s):
        k = class_of(s)
        encode(last(s), zsend.at[k], zsscale.at[k])
        for copy in z_copies(k, (c - k + 3) % 4):
            copy.start()

    def middle(i, carry):
        give(0, class_of(i))
        step(EARLY + 4 + i, carry)
        hand_in(i)
        return carry

    lax.fori_loop(0, 2, middle, 0)
    step(STEPS + 1, 0)
    give(0, class_of(2))
    give(0, class_of(3))
    hand_in(2)
    own[...] = last(3)

    total = own[...]
    for slot in range(3):
        for copy in z_copies((c + 1) % 4, slot):
            copy.wait_recv()
        total = total + decode(zrecv[slot], zrscale[slot])
    own[...] = total
    for p in range(PB):
        turned = own[p * BLOCK : (p + 1) * BLOCK, :].T
        out[0, p, :, 0:BLOCK] = turned[0:BLOCK]
        out[0, p, :, BLOCK:128] = turned[BLOCK:128]

    def sent(u, carry):
        hand(u).wait_send()
        for copy in part_copies(u):
            copy.wait_send()
        return carry

    lax.fori_loop(0, STEPS, sent, 0)
    for copy in weights():
        copy.wait_send()
    for way in range(2):
        for part in range(2):
            halo(way, part).wait_send()
    for n in range(8):
        core_copy(n).wait_send()
    for n in range(4):
        for copy in x_copies(n):
            copy.wait_send()
    for n in range(1, 4):
        for copy in z_copies((c + n) % 4, 0):
            copy.wait_send()


def body(green, broadening, quad_weight, pair_cols):
    vmem, smem = pl.BlockSpec(memory_space=pltpu.VMEM), pl.BlockSpec(memory_space=pltpu.SMEM)
    hbm = pl.BlockSpec(memory_space=pl.ANY)
    dma = pltpu.SemaphoreType.DMA
    return pl.pallas_call(
        kernel,
        out_shape=jax.ShapeDtypeStruct((1, PB, BLOCK, 2 * BLOCK), jnp.float32),
        in_specs=[hbm, hbm, smem, smem],
        out_specs=vmem,
        scratch_shapes=[
            pltpu.VMEM((2, 16, BLOCK, 1024), jnp.bfloat16),
            pltpu.VMEM((2, 48, BLOCK, 256), jnp.bfloat16),
            pltpu.VMEM((2, 48, BLOCK, 256), jnp.bfloat16),
            pltpu.VMEM((8, 1024, 128), jnp.float32),
            pltpu.VMEM((2, 1024, 512), jnp.bfloat16),
            pltpu.VMEM((2, 1024, 512), jnp.bfloat16),
            pltpu.VMEM((2, 512, 512), jnp.bfloat16),
            pltpu.VMEM((2, 256, 512), jnp.bfloat16),
            pltpu.VMEM((16, 128, 1024), jnp.bfloat16),
            pltpu.VMEM((STEPS, BLOCK, 1024), jnp.int16),
            pltpu.VMEM((STEPS, BLOCK, 1024), jnp.int16),
            pltpu.VMEM((STEPS, 8, 128), jnp.float32),
            pltpu.VMEM((STEPS, 8, 128), jnp.float32),
            pltpu.VMEM((8, 1024, 128), jnp.float32),
            pltpu.VMEM((8, 1024, 128), jnp.float32),
            pltpu.VMEM((4, 1024, 128), jnp.int16),
            pltpu.VMEM((4, 1024, 128), jnp.int16),
            pltpu.VMEM((4, 8, 128), jnp.float32),
            pltpu.VMEM((4, 8, 128), jnp.float32),
            pltpu.VMEM((4, 1024, 128), jnp.int16),
            pltpu.VMEM((3, 1024, 128), jnp.int16),
            pltpu.VMEM((4, 8, 128), jnp.float32),
            pltpu.VMEM((3, 8, 128), jnp.float32),
            pltpu.VMEM((1024, 128), jnp.float32),
            dma((6,)), dma((2,)), dma((2,)),
            dma((STEPS,)), dma((STEPS,)), dma((STEPS,)), dma((STEPS,)), dma((STEPS,)), dma((STEPS,)),
            dma((2, 2)), dma((2, 2)),
            dma((8,)), dma((8,)),
            dma((4,)), dma((4,)), dma((4,)), dma((4,)),
            dma((4,)), dma((3,)), dma((4,)), dma((3,)),
        ],
        compiler_params=pltpu.CompilerParams(
            collective_id=0, has_side_effects=True, vmem_limit_bytes=56 * 1024 * 1024
        ),
        cost_estimate=pl.CostEstimate(flops=13 * 10**9, bytes_accessed=7 * 2**20, transcendentals=0),
        name="density",
    )(green.reshape(1, 2, 16, BLOCK, 512), broadening, quad_weight, pair_cols)


def solution(mesh):
    placed = (
        P("energy", None, "row", "col"),
        P("energy", None, None, "col"),
        P("energy"),
        P("row"),
    )
    return jax.shard_map(
        body,
        mesh=mesh,
        in_specs=placed,
        out_specs=P("row", ("energy", "col"), None, None),
        check_vma=False,
    )
```

time: 111 us -> 97 us (0.87)
  Pallas kernels: 107 us -> 93.6 us
    pallas_call x1, Pallas kernels: 107 us -> 93.6 us  [body(): pl.pallas_call(kernel, out_shape=jax.ShapeDtypeStruct((1, PB, BLOCK, 2 *...]
where the time goes in v2:
time: 97 us; the launch traced here: 96.2 us
  Pallas kernels  93.6 us (96%)
  local copies, waits for them, and re-layouts  1.89 us (2%)
    pallas_call x1, Pallas kernels, body(): pl.pallas_call(kernel, out_shape=jax.ShapeDtypeStruct((1, PB, BLOCK, 2 *...  93.6 us

profile of v2, /device:TPU:96, one launch (start us, length us, event | category | flops | bytes accessed | tf_op | source)
XLA Modules:
  0.0 96.2 jit_solution(13569207958804224576)
XLA Ops:
  0.7 93.6 %density.1 = f32[1,16,64,128]{3,2,1,0:T(8,128)} custom-call(bf16[1,2,16,64,512]{4,3,2,1,0:T(8,128)(2,1)} %bitcast.1, bf16[1,2,2048,512]{3,2,1,0:T(8,128)(2,1)} %gamma.1, f32[1]{0:T(128)S(6)} %copy.6.weight, s32[256]{0:T(256)} %pairs.1), custom_call_target="tpu_custom_call" | custom-call | flops 12999999488 | bytes 7340032 | tf_op jit(solution)/shard_map/density/pallas_call | solution.py:309
  94.3 1.9 %copy.7 = f32[1,16,64,128]{3,2,1,0:T(8,128)} copy(f32[1,16,64,128]{3,2,1,0:T(8,128)} %density.1) | data formatting | bytes 1048576

commit v3 on v2

--- a/solution.py
+++ b/solution.py
@@ -39,8 +39,8 @@
 def kernel(
     green, gamma, weight, pairs, out,
     held, near_a, near_b, begun, mine, theirs, turn, given, spec, psend, precv, psscale, prscale,
-    csend, crecv, xsend, xrecv, xsscale, xrscale, zsend, zrecv, zsscale, zrscale, own,
-    loc, ws, wr, gs, gr, ps, pr, pss, prs, ys, yr, cs, cr, xs, xr, xss, xrs, zs, zr, zss, zrs,
+    csend, crecv, csscale, crscale, xsend, xrecv, xsscale, xrscale, zsend, zrecv, zsscale, zrscale, own,
+    loc, ws, wr, gs, gr, ps, pr, pss, prs, ys, yr, cs, cr, css, crs, xs, xr, xss, xrs, zs, zr, zss, zrs,
 ):
     near = (near_a, near_b)
     e, r, c = lax.axis_index("energy"), lax.axis_index("row"), lax.axis_index("col")
@@ -54,7 +54,7 @@
         return pl.ds(pl.multiple_of(owner * 512, 512), count)
 
     def block_of(u):
-        dx, dk, k = 1 - u // 8, 1 - u % 2, (u % 8) // 2
+        dx, dk, k = 1 - u // 8, 1 - (u // 4) % 2, u % 4
         return ((xbit + dx) % 2) * 8 + ((core + dk) % 2) * 4 + k
 
     def remote(src, dst, send, recv, peer):
@@ -89,8 +89,11 @@
             ys.at[way, part], yr.at[way, part], (e, (above, below)[way], c),
         )
 
-    def core_copy(n):
-        return remote(csend.at[n], crecv.at[n], cs.at[n], cr.at[n], core_peer)
+    def core_copies(n):
+        return (
+            remote(csend.at[n], crecv.at[n], cs.at[n], cr.at[n], core_peer),
+            remote(csscale.at[n], crscale.at[n], css.at[n], crs.at[n], core_peer),
+        )
 
     def x_copies(n):
         return (
@@ -125,8 +128,23 @@
         copy.start()
     for u in range(LEAD):
         hand(u).start()
-    for way in range(2):
-        halo(way, 0).start()
+
+    def sends(way):
+        return r < 7 if way == 0 else r > 0
+
+    def halo_start(part):
+        for way in range(2):
+            @pl.when(sends(way))
+            def _():
+                halo(way, part).start()
+
+    def halo_wait(part):
+        for way in range(2):
+            @pl.when(sends(1 - way))
+            def _():
+                halo(way, part).wait_recv()
+
+    halo_start(0)
     for copy in locals_:
         copy.wait()
     theirs[0, 0:512, :] = turn[0].T
@@ -183,20 +201,22 @@
         return found + lax.dot_general(right_im, left_im, NT, preferred_element_type=jnp.float32)
 
     def both(dx, dk, k):
-        n = 2 * k + 1 - dk
+        n = (1 - dk) * 4 + k
         first = begun[n] if dx else terms(dx, dk, k, 0)
         return (first + terms(dx, dk, k, 1)) * weight[0]
 
     def give(dx, k):
         n = (1 - dx) * 4 + k
-        csend[n] = both(dx, 1, k)
-        core_copy(n).start()
+        encode(both(dx, 1, k), csend.at[n], csscale.at[n])
+        for copy in core_copies(n):
+            copy.start()
 
     def kept(dx, k):
         n = (1 - dx) * 4 + k
         found = both(dx, 0, k)
-        core_copy(n).wait_recv()
-        return found + crecv[n]
+        for copy in core_copies(n):
+            copy.wait_recv()
+        return found + decode(crecv[n], crscale[n])
 
     def class_of(s):
         return jnp.where(s == 3, c, jnp.where(s < c, s, s + 1))
@@ -215,21 +235,19 @@
     def step_and_begin(u, carry):
         step(u, carry)
         n = u - 3
-        begun[n] = terms(1, 1 - n % 2, n // 2, 0)
+        begun[n] = terms(1, 1 - n // 4, n % 4, 0)
         return carry
 
     lax.fori_loop(0, 2, step, 0)
-    for way in range(2):
-        halo(way, 1).start()
+    halo_start(1)
     lax.fori_loop(2, 3, step, 0)
-    for way in range(2):
-        halo(way, 0).wait_recv()
+    halo_wait(0)
     lax.fori_loop(3, EARLY, step_and_begin, 0)
-    for way in range(2):
-        halo(way, 1).wait_recv()
+    halo_wait(1)
     give(1, class_of(0))
 
     def early(s, carry):
+        step(EARLY + s, carry)
         k = class_of(s)
 
         @pl.when(s < 3)
@@ -239,7 +257,7 @@
         encode(kept(1, k), xsend.at[k], xsscale.at[k])
         for copy in x_copies(k):
             copy.start()
-        return step(EARLY + s, carry)
+        return carry
 
     lax.fori_loop(0, 4, early, 0)
 
@@ -258,15 +276,21 @@
 
     def middle(i, carry):
         give(0, class_of(i))
-        step(EARLY + 4 + i, carry)
-        hand_in(i)
-        return carry
-
-    lax.fori_loop(0, 2, middle, 0)
+
+        @pl.when(i < 2)
+        def _():
+            step(EARLY + 4 + i, 0)
+
+        @pl.when(i > 0)
+        def _():
+            hand_in(i - 1)
+
+        return carry
+
+    lax.fori_loop(0, 3, middle, 0)
     step(STEPS + 1, 0)
-    give(0, class_of(2))
-    give(0, class_of(3))
     hand_in(2)
+    give(0, c)
     own[...] = last(3)
 
     total = own[...]
@@ -290,10 +314,13 @@
     for copy in weights():
         copy.wait_send()
     for way in range(2):
-        for part in range(2):
-            halo(way, part).wait_send()
+        @pl.when(sends(way))
+        def _():
+            for part in range(2):
+                halo(way, part).wait_send()
     for n in range(8):
-        core_copy(n).wait_send()
+        for copy in core_copies(n):
+            copy.wait_send()
     for n in range(4):
         for copy in x_copies(n):
             copy.wait_send()
@@ -325,8 +352,10 @@
             pltpu.VMEM((STEPS, BLOCK, 1024), jnp.int16),
             pltpu.VMEM((STEPS, 8, 128), jnp.float32),
             pltpu.VMEM((STEPS, 8, 128), jnp.float32),
-            pltpu.VMEM((8, 1024, 128), jnp.float32),
-            pltpu.VMEM((8, 1024, 128), jnp.float32),
+            pltpu.VMEM((8, 1024, 128), jnp.int16),
+            pltpu.VMEM((8, 1024, 128), jnp.int16),
+            pltpu.VMEM((8, 8, 128), jnp.float32),
+            pltpu.VMEM((8, 8, 128), jnp.float32),
             pltpu.VMEM((4, 1024, 128), jnp.int16),
             pltpu.VMEM((4, 1024, 128), jnp.int16),
             pltpu.VMEM((4, 8, 128), jnp.float32),
@@ -339,7 +368,7 @@
             dma((6,)), dma((2,)), dma((2,)),
             dma((STEPS,)), dma((STEPS,)), dma((STEPS,)), dma((STEPS,)), dma((STEPS,)), dma((STEPS,)),
             dma((2, 2)), dma((2, 2)),
-            dma((8,)), dma((8,)),
+            dma((8,)), dma((8,)), dma((8,)), dma((8,)),
             dma((4,)), dma((4,)), dma((4,)), dma((4,)),
             dma((4,)), dma((3,)), dma((4,)), dma((3,)),
         ],

time: 97 us -> 92.3 us (0.952)
  Pallas kernels: 93.6 us -> 89.6 us
    pallas_call x1, Pallas kernels: 93.6 us -> 89.6 us  [body(): pl.pallas_call(kernel, out_shape=jax.ShapeDtypeStruct((1, PB, BLOCK, 2 *...]
where the time goes in v3:
time: 92.3 us; the launch traced here: 92.1 us
  Pallas kernels  89.6 us (97%)
  local copies, waits for them, and re-layouts  1.89 us (2%)
    pallas_call x1, Pallas kernels, body(): pl.pallas_call(kernel, out_shape=jax.ShapeDtypeStruct((1, PB, BLOCK, 2 *...  89.6 us
    unnamed x1, local copies, waits for them, and re-layouts  1.89 us

profile of v3, /device:TPU:96, one launch (start us, length us, event | category | flops | bytes accessed | tf_op | source)
XLA Modules:
  0.0 92.1 jit_solution(11363164154720720411)
XLA Ops:
  0.7 89.6 %density.1 = f32[1,16,64,128]{3,2,1,0:T(8,128)} custom-call(bf16[1,2,16,64,512]{4,3,2,1,0:T(8,128)(2,1)} %bitcast.1, bf16[1,2,2048,512]{3,2,1,0:T(8,128)(2,1)} %gamma.1, f32[1]{0:T(128)S(6)} %copy.6.weight, s32[256]{0:T(256)} %pairs.1), custom_call_target="tpu_custom_call" | custom-call | flops 12999999488 | bytes 7340032 | tf_op jit(solution)/shard_map/density/pallas_call | solution.py:336
  90.3 1.9 %copy.7 = f32[1,16,64,128]{3,2,1,0:T(8,128)} copy(f32[1,16,64,128]{3,2,1,0:T(8,128)} %density.1) | data formatting | bytes 1048576

commit v4 on v3

--- a/solution.py
+++ b/solution.py
@@ -11,36 +11,30 @@
 NT = (((1,), (1,)), ((), ()))
 BLOCK = 64
 PB = 16
-TOP = 32766.0
+TOP = 32000.0
 STEPS = 16
 LEAD = 3
 EARLY = 11
 
 
-def scaled(total, peak):
-    peak = jnp.maximum(peak, 1e-30)
-    return total * (TOP / peak), peak * (1.0 / TOP)
-
-
-def coded(values):
-    return jnp.round(values).astype(jnp.int32).astype(jnp.int16)
-
-
-def encode(total, codes, scale):
-    values, unit = scaled(total, jnp.max(jnp.abs(total), axis=0, keepdims=True))
-    codes[...] = coded(values)
-    scale[...] = jnp.broadcast_to(unit, scale.shape)
-
-
-def decode(codes, scale):
-    return codes[...].astype(jnp.int32).astype(jnp.float32) * scale[0:1, :]
+def encode(total, codes):
+    rows = total.shape[0]
+    power = jnp.ceil(jnp.log2(jnp.maximum(jnp.max(jnp.abs(total), axis=0, keepdims=True), 1e-30)))
+    codes[0:rows] = jnp.round(total * (TOP * jnp.exp2(-power))).astype(jnp.int32).astype(jnp.int16)
+    codes[rows : rows + 16] = jnp.broadcast_to(power, (16, 128)).astype(jnp.int32).astype(jnp.int16)
+
+
+def decode(codes):
+    rows = codes.shape[0] - 16
+    power = codes[rows:][0:1].astype(jnp.int32).astype(jnp.float32)
+    return codes[0:rows].astype(jnp.int32).astype(jnp.float32) * (jnp.exp2(power) * (1.0 / TOP))
 
 
 def kernel(
     green, gamma, weight, pairs, out,
-    held, near_a, near_b, begun, mine, theirs, turn, given, spec, psend, precv, psscale, prscale,
-    csend, crecv, csscale, crscale, xsend, xrecv, xsscale, xrscale, zsend, zrecv, zsscale, zrscale, own,
-    loc, ws, wr, gs, gr, ps, pr, pss, prs, ys, yr, cs, cr, css, crs, xs, xr, xss, xrs, zs, zr, zss, zrs,
+    held, near_a, near_b, begun, mine, theirs, turn, given, spec, psend, precv,
+    csend, crecv, xsend, xrecv, zsend, zrecv, own,
+    loc, ws, wr, gs, gr, ps, pr, ys, yr, cs, cr, xs, xr, zs, zr,
 ):
     near = (near_a, near_b)
     e, r, c = lax.axis_index("energy"), lax.axis_index("row"), lax.axis_index("col")
@@ -80,7 +74,6 @@
     def part_copies(u):
         return (
             remote(psend.at[u], precv.at[u], ps.at[u], pr.at[u], pair_peer),
-            remote(psscale.at[u], prscale.at[u], pss.at[u], prs.at[u], pair_peer),
         )
 
     def halo(way, part):
@@ -92,19 +85,16 @@
     def core_copies(n):
         return (
             remote(csend.at[n], crecv.at[n], cs.at[n], cr.at[n], core_peer),
-            remote(csscale.at[n], crscale.at[n], css.at[n], crs.at[n], core_peer),
         )
 
     def x_copies(n):
         return (
             remote(xsend.at[n], xrecv.at[n], xs.at[n], xr.at[n], x_peer),
-            remote(xsscale.at[n], xrscale.at[n], xss.at[n], xrs.at[n], x_peer),
         )
 
     def z_copies(k, slot):
         return (
             remote(zsend.at[k], zrecv.at[slot], zs.at[k], zr.at[slot], (e, r, k)),
-            remote(zsscale.at[k], zrscale.at[slot], zss.at[k], zrs.at[slot], (e, r, k)),
         )
 
     locals_ = [
@@ -169,12 +159,7 @@
 
         hand(u).wait_recv()
         part = product(block_of(u), theirs)
-        peak = jnp.max(jnp.abs(part), axis=0, keepdims=True)
-        peak = functools.reduce(jnp.maximum, [peak[:, 128 * i : 128 * (i + 1)] for i in range(8)])
-        wide = jnp.concatenate([peak] * 8, axis=1)
-        values, unit = scaled(part, wide)
-        psend[u] = coded(values)
-        psscale[u] = jnp.broadcast_to(unit[:, 0:128], (8, 128))
+        encode(jnp.concatenate([part[:, 128 * i : 128 * (i + 1)] for i in range(8)], axis=0), psend.at[u])
         for copy in part_copies(u):
             copy.start()
 
@@ -183,8 +168,8 @@
         part = product(b, mine)
         for copy in part_copies(u):
             copy.wait_recv()
-        unit = jnp.concatenate([prscale[u][0:1, :]] * 8, axis=1)
-        whole = part + precv[u].astype(jnp.int32).astype(jnp.float32) * unit
+        other = decode(precv.at[u])
+        whole = part + jnp.concatenate([other[BLOCK * i : BLOCK * (i + 1)] for i in range(8)], axis=1)
         whole = whole.astype(jnp.bfloat16)
         spec[b, 0:BLOCK, :] = whole
         spec[b, BLOCK:128, 0:512] = whole[:, 512:]
@@ -207,7 +192,7 @@
 
     def give(dx, k):
         n = (1 - dx) * 4 + k
-        encode(both(dx, 1, k), csend.at[n], csscale.at[n])
+        encode(both(dx, 1, k), csend.at[n])
         for copy in core_copies(n):
             copy.start()
 
@@ -216,7 +201,7 @@
         found = both(dx, 0, k)
         for copy in core_copies(n):
             copy.wait_recv()
-        return found + decode(crecv[n], crscale[n])
+        return found + decode(crecv.at[n])
 
     def class_of(s):
         return jnp.where(s == 3, c, jnp.where(s < c, s, s + 1))
@@ -254,7 +239,7 @@
         def _():
             give(1, class_of(s + 1))
 
-        encode(kept(1, k), xsend.at[k], xsscale.at[k])
+        encode(kept(1, k), xsend.at[k])
         for copy in x_copies(k):
             copy.start()
         return carry
@@ -266,11 +251,11 @@
         total = kept(0, k)
         for copy in x_copies(k):
             copy.wait_recv()
-        return total + decode(xrecv[k], xrscale[k])
+        return total + decode(xrecv.at[k])
 
     def hand_in(s):
         k = class_of(s)
-        encode(last(s), zsend.at[k], zsscale.at[k])
+        encode(last(s), zsend.at[k])
         for copy in z_copies(k, (c - k + 3) % 4):
             copy.start()
 
@@ -297,7 +282,7 @@
     for slot in range(3):
         for copy in z_copies((c + 1) % 4, slot):
             copy.wait_recv()
-        total = total + decode(zrecv[slot], zrscale[slot])
+        total = total + decode(zrecv.at[slot])
     own[...] = total
     for p in range(PB):
         turned = own[p * BLOCK : (p + 1) * BLOCK, :].T
@@ -348,29 +333,21 @@
             pltpu.VMEM((2, 512, 512), jnp.bfloat16),
             pltpu.VMEM((2, 256, 512), jnp.bfloat16),
             pltpu.VMEM((16, 128, 1024), jnp.bfloat16),
-            pltpu.VMEM((STEPS, BLOCK, 1024), jnp.int16),
-            pltpu.VMEM((STEPS, BLOCK, 1024), jnp.int16),
-            pltpu.VMEM((STEPS, 8, 128), jnp.float32),
-            pltpu.VMEM((STEPS, 8, 128), jnp.float32),
-            pltpu.VMEM((8, 1024, 128), jnp.int16),
-            pltpu.VMEM((8, 1024, 128), jnp.int16),
-            pltpu.VMEM((8, 8, 128), jnp.float32),
-            pltpu.VMEM((8, 8, 128), jnp.float32),
-            pltpu.VMEM((4, 1024, 128), jnp.int16),
-            pltpu.VMEM((4, 1024, 128), jnp.int16),
-            pltpu.VMEM((4, 8, 128), jnp.float32),
-            pltpu.VMEM((4, 8, 128), jnp.float32),
-            pltpu.VMEM((4, 1024, 128), jnp.int16),
-            pltpu.VMEM((3, 1024, 128), jnp.int16),
-            pltpu.VMEM((4, 8, 128), jnp.float32),
-            pltpu.VMEM((3, 8, 128), jnp.float32),
+            pltpu.VMEM((STEPS, 528, 128), jnp.int16),
+            pltpu.VMEM((STEPS, 528, 128), jnp.int16),
+            pltpu.VMEM((8, 1040, 128), jnp.int16),
+            pltpu.VMEM((8, 1040, 128), jnp.int16),
+            pltpu.VMEM((4, 1040, 128), jnp.int16),
+            pltpu.VMEM((4, 1040, 128), jnp.int16),
+            pltpu.VMEM((4, 1040, 128), jnp.int16),
+            pltpu.VMEM((3, 1040, 128), jnp.int16),
             pltpu.VMEM((1024, 128), jnp.float32),
             dma((6,)), dma((2,)), dma((2,)),
-            dma((STEPS,)), dma((STEPS,)), dma((STEPS,)), dma((STEPS,)), dma((STEPS,)), dma((STEPS,)),
+            dma((STEPS,)), dma((STEPS,)), dma((STEPS,)), dma((STEPS,)),
             dma((2, 2)), dma((2, 2)),
-            dma((8,)), dma((8,)), dma((8,)), dma((8,)),
-            dma((4,)), dma((4,)), dma((4,)), dma((4,)),
-            dma((4,)), dma((3,)), dma((4,)), dma((3,)),
+            dma((8,)), dma((8,)),
+            dma((4,)), dma((4,)),
+            dma((4,)), dma((3,)),
         ],
         compiler_params=pltpu.CompilerParams(
             collective_id=0, has_side_effects=True, vmem_limit_bytes=56 * 1024 * 1024

time: 92.3 us -> 91.8 us (level)
  no operation moved by 1% of the time
where the time goes in v4:
time: 91.8 us; the launch traced here: 91.6 us
  Pallas kernels  89.1 us (97%)
  local copies, waits for them, and re-layouts  1.89 us (2%)
    pallas_call x1, Pallas kernels, body(): pl.pallas_call(kernel, out_shape=jax.ShapeDtypeStruct((1, PB, BLOCK, 2 *...  89.1 us
    unnamed x1, local copies, waits for them, and re-layouts  1.89 us

profile of v4, /device:TPU:96, one launch (start us, length us, event | category | flops | bytes accessed | tf_op | source)
XLA Modules:
  0.0 91.6 jit_solution(10624387244008268206)
XLA Ops:
  0.7 89.1 %density.1 = f32[1,16,64,128]{3,2,1,0:T(8,128)} custom-call(bf16[1,2,16,64,512]{4,3,2,1,0:T(8,128)(2,1)} %bitcast.1, bf16[1,2,2048,512]{3,2,1,0:T(8,128)(2,1)} %gamma.1, f32[1]{0:T(128)S(6)} %copy.6.weight, s32[256]{0:T(256)} %pairs.1), custom_call_target="tpu_custom_call" | custom-call | flops 12999999488 | bytes 7340032 | tf_op jit(solution)/shard_map/density/pallas_call | solution.py:321
  89.7 1.9 %copy.7 = f32[1,16,64,128]{3,2,1,0:T(8,128)} copy(f32[1,16,64,128]{3,2,1,0:T(8,128)} %density.1) | data formatting | bytes 1048576
